TPU v7x, 32 devices: a whole 2x2x4 slice. The times are simulated.
32 devices in a mesh: row: 8 (over y, x, core), col: 4 (over z).
Axes of the slice: x: 2, y: 2, z: 4, core: 2. Of those that a mesh axis runs over, the one named last changes fastest.
Arguments:
- inputs: bfloat16 [512, 6144], P('row', 'col'), may hold values from -6 to 6
- cotangent: bfloat16 [512, 6144], P('row', 'col'), may hold values from -6 to 6
- w_in: bfloat16 [6144, 12288], P('col', 'row'), may hold values from -0.078125 to 0.078125
- w_out: bfloat16 [12288, 6144], P('row', 'col'), may hold values from -0.0546875 to 0.0546875
Outputs:
- grad_inputs: bfloat16 [512, 6144], P('row', 'col')
- grad_w_in: bfloat16 [6144, 12288], P('col', 'row')
- grad_w_out: bfloat16 [12288, 6144], P('row', 'col')
All inputs are finite; a program needn't handle non-finite values.
Results may differ from a plain program's by a relative error of at most 0.017.
Values may be sent and summed in bfloat16 or wider, within the bound.
A program may use at most 128 MiB of HBM per device.

v0:
```python
import math

import jax
import jax.numpy as jnp
from jax import lax
from jax.sharding import PartitionSpec as P

cubic_coef = 0.044715
tanh_scale = math.sqrt(2.0 / math.pi)


def activate(pre, back):
    inner = tanh_scale * (pre + cubic_coef * pre * pre * pre)
    tval = jnp.tanh(inner)
    act = (0.5 * pre * (1.0 + tval)).astype(jnp.bfloat16)
    deriv = 0.5 * (1.0 + tval) + 0.5 * pre * (1.0 - tval * tval) * tanh_scale * (
        1.0 + 3.0 * cubic_coef * pre * pre
    )
    slope = (back * deriv).astype(jnp.bfloat16)
    return (act, slope)


def on_device(inputs, cotangent, w_in, w_out):
    whole_in, whole_cot = (
        lax.all_gather(inputs, "row", axis=0, tiled=True),
        lax.all_gather(cotangent, "row", axis=0, tiled=True),
    )
    pre_part = jnp.dot(whole_in, w_in, preferred_element_type=jnp.float32).astype(jnp.bfloat16)
    back_part = lax.dot_general(
        whole_cot, w_out, (((1,), (1,)), ((), ())), preferred_element_type=jnp.float32
    ).astype(jnp.bfloat16)
    groups = lax.axis_size("col")
    total_rows = pre_part.shape[0]
    share_rows = total_rows // groups
    hidden_width = pre_part.shape[1]
    pre_blocks = pre_part.reshape(groups, share_rows, hidden_width)
    back_blocks = back_part.reshape(groups, share_rows, hidden_width)
    pre_recv, back_recv = (
        lax.all_to_all(pre_blocks, "col", split_axis=0, concat_axis=0, tiled=True),
        lax.all_to_all(back_blocks, "col", split_axis=0, concat_axis=0, tiled=True),
    )
    pre_share = jnp.sum(pre_recv.astype(jnp.float32), axis=0)
    back_share = jnp.sum(back_recv.astype(jnp.float32), axis=0)
    act_share, slope_share = activate(pre_share, back_share)
    act_all, slope_all = (
        lax.all_gather(act_share, "col", axis=0, tiled=True),
        lax.all_gather(slope_share, "col", axis=0, tiled=True),
    )
    grad_inputs = lax.psum_scatter(
        lax.dot_general(
            slope_all, w_in, (((1,), (1,)), ((), ())), preferred_element_type=jnp.float32
        ).astype(jnp.bfloat16),
        "row",
        scatter_dimension=0,
        tiled=True,
    )
    grad_w_in = lax.dot_general(
        whole_in, slope_all, (((0,), (0,)), ((), ())), preferred_element_type=jnp.float32
    ).astype(jnp.bfloat16)
    grad_w_out = lax.dot_general(
        act_all, whole_cot, (((0,), (0,)), ((), ())), preferred_element_type=jnp.float32
    ).astype(jnp.bfloat16)
    return (grad_inputs, grad_w_in, grad_w_out)


def solution(mesh):
    return jax.shard_map(
        on_device,
        mesh=mesh,
        in_specs=(P("row", "col"), P("row", "col"), P("col", "row"), P("row", "col")),
        out_specs=(P("row", "col"), P("col", "row"), P("row", "col")),
        check_vma=False,
    )
```

profile of v0, /device:TPU:1, one launch (start us, length us, event | category | flops | bytes accessed | tf_op | source)
XLA Modules:
  0.0 248.4 jit_solution(7246016786524279165)
XLA Ops:
  7.2 0.0 all-gather.5.cloned.1.call-start
  7.2 0.7 all-gather.5.cloned.1.call-update
  7.9 0.0 all-gather.7.cloned.1.call-start
  7.9 0.7 all-gather.7.cloned.1.call-update
  8.6 29.5 %all-gather.5.cloned.1.call-done = bf16[512,1536]{1,0:T(8,128)(2,1)} async-done(((bf16[64,1536]{1,0:T(8,128)(2,1)}), bf16[512,1536]{1,0:T(8,128)(2,1)}) %all-gather.5.cloned.1.call-update) | async-done | bytes 1572880 | tf_op jit(solution)/shard_map/all_gather | solution.py:26
  38.1 6.6 %convolution_convert_fusion.4 = bf16[512,1536]{1,0:T(8,128)(2,1)} fusion(bf16[512,1536]{1,0:T(8,128)(2,1)} %all-gather.5.cloned.1.call-done, bf16[1536,1536]{1,0:T(8,128)(2,1)} %param.7), kind=kOutput, calls=%fused_computation.7 | convolution fusion | flops 2416705536 | bytes 7864320 | tf_op jit(solution)/shard_map/dot_general | solution.py:29
  44.7 4.3 %all-to-all-start = ((bf16[4,128,1536]{2,1,0:T(8,128)(2,1)}), bf16[4,128,1536]{2,1,0:T(8,128)(2,1)S(1)}, u32[]{:S(2)}, u32[]{:S(2)}) async-start(bf16[4,128,1536]{2,1,0:T(8,128)(2,1)} %bitcast), calls=%async_computation | async-start | bytes 3145728 | tf_op jit(solution)/shard_map/all_to_all | solution.py:40
  49.0 16.7 %all-gather.7.cloned.1.call-done = bf16[512,1536]{1,0:T(8,128)(2,1)} async-done(((bf16[64,1536]{1,0:T(8,128)(2,1)}), bf16[512,1536]{1,0:T(8,128)(2,1)}) %all-gather.7.cloned.1.call-update) | async-done | bytes 1572880 | tf_op jit(solution)/shard_map/all_gather | solution.py:25
  65.7 6.6 %convolution_convert_fusion.3 = bf16[512,1536]{1,0:T(8,128)(2,1)} fusion(bf16[512,1536]{1,0:T(8,128)(2,1)} %all-gather.7.cloned.1.call-done, bf16[1536,1536]{1,0:T(8,128)(2,1)} %param.6), kind=kOutput, calls=%fused_computation.6 | convolution fusion | flops 2416705536 | bytes 7864320 | tf_op jit(solution)/shard_map/dot_general | solution.py:28
  72.3 13.3 %all-to-all-done = bf16[4,128,1536]{2,1,0:T(8,128)(2,1)S(1)} async-done(((bf16[4,128,1536]{2,1,0:T(8,128)(2,1)}), bf16[4,128,1536]{2,1,0:T(8,128)(2,1)S(1)}, u32[]{:S(2)}, u32[]{:S(2)}) %all-to-all-start) | async-done | bytes 1572896 | tf_op jit(solution)/shard_map/all_to_all | solution.py:40
  85.6 3.6 %all-to-all-start.1 = ((bf16[4,128,1536]{2,1,0:T(8,128)(2,1)}), bf16[4,128,1536]{2,1,0:T(8,128)(2,1)S(1)}, u32[]{:S(2)}, u32[]{:S(2)}) async-start(bf16[4,128,1536]{2,1,0:T(8,128)(2,1)} %bitcast.14), calls=%async_computation.1 | async-start | bytes 3145728 | tf_op jit(solution)/shard_map/all_to_all | solution.py:39
  89.2 0.0 all-gather.9.cloned.1.call-start
  89.2 1.1 convert_reduce_fusion.1
  90.3 0.0 copy-start
  90.3 35.3 %all-to-all-done.1 = bf16[4,128,1536]{2,1,0:T(8,128)(2,1)S(1)} async-done(((bf16[4,128,1536]{2,1,0:T(8,128)(2,1)}), bf16[4,128,1536]{2,1,0:T(8,128)(2,1)S(1)}, u32[]{:S(2)}, u32[]{:S(2)}) %all-to-all-start.1) | async-done | bytes 1572896 | tf_op jit(solution)/shard_map/all_to_all | solution.py:39
  125.6 0.2 convert_reduce_fusion
  125.8 0.0 copy-done
  125.8 1.4 multiply_convert_fusion
  127.2 0.0 all-gather.9.cloned.1.call-update
  127.2 0.0 all-gather.11.cloned.1.call-start
  127.3 0.5 all-gather.11.cloned.1.call-update
  127.8 0.0 reduce-scatter.2.cloned.1.call-start
  127.9 35.4 %all-gather.9.cloned.1.call-done = bf16[512,1536]{1,0:T(8,128)(2,1)} async-done(((bf16[128,1536]{1,0:T(8,128)(2,1)}), bf16[512,1536]{1,0:T(8,128)(2,1)}) %all-gather.9.cloned.1.call-update) | async-done | bytes 1572880 | tf_op jit(solution)/shard_map/all_gather | solution.py:47
  163.3 0.0 copy-start.3
  163.3 6.7 %convolution_convert_fusion.2 = bf16[512,1536]{1,0:T(8,128)(2,1)} fusion(bf16[512,1536]{1,0:T(8,128)(2,1)} %all-gather.9.cloned.1.call-done, bf16[1536,1536]{1,0:T(8,128)(2,1)} %param.6), kind=kOutput, calls=%fused_computation.5 | convolution fusion | flops 2416705536 | bytes 7864320 | tf_op jit(solution)/shard_map/dot_general | solution.py:50
  170.0 0.0 copy-start.2
  170.0 0.0 reduce-scatter.2.cloned.1.call-update
  170.1 0.0 copy-done.3
  170.1 1.4 copy-done.2
  171.5 4.3 %fusion = bf16[1536,1536]{0,1:T(8,128)(2,1)} fusion(bf16[512,1536]{1,0:T(8,128)(2,1)S(1)} %copy-done.3, bf16[512,1536]{1,0:T(8,128)(2,1)S(1)} %copy-done.2), kind=kOutput, calls=%fused_computation.2 | convolution fusion | flops 2418278400 | bytes 7864320 | tf_op jit(solution)/shard_map/dot_general | solution.py:57
  175.8 0.0 copy-start.1
  175.8 6.7 %copy.7 = bf16[1536,1536]{1,0:T(8,128)(2,1)} copy(bf16[1536,1536]{0,1:T(8,128)(2,1)} %fusion) | data formatting | bytes 9437184
  182.5 18.2 %all-gather.11.cloned.1.call-done = bf16[512,1536]{1,0:T(8,128)(2,1)} async-done(((bf16[128,1536]{1,0:T(8,128)(2,1)}), bf16[512,1536]{1,0:T(8,128)(2,1)}) %all-gather.11.cloned.1.call-update) | async-done | bytes 1572880 | tf_op jit(solution)/shard_map/all_gather | solution.py:46
  200.7 0.0 copy-done.1
  200.7 5.7 %convolution_convert_fusion = bf16[1536,1536]{1,0:T(8,128)(2,1)} fusion(bf16[512,1536]{1,0:T(8,128)(2,1)} %all-gather.11.cloned.1.call-done, bf16[512,1536]{1,0:T(8,128)(2,1)S(1)} %copy-done.1), kind=kOutput, calls=%fused_computation | convolution fusion | flops 2418278400 | bytes 7864320 | tf_op jit(solution)/shard_map/dot_general | solution.py:60
  206.4 35.5 %reduce-scatter.2.cloned.1.call-done = bf16[64,1536]{1,0:T(8,128)(2,1)} async-done(((bf16[512,1536]{1,0:T(8,128)(2,1)}), bf16[64,1536]{1,0:T(8,128)(2,1)}) %reduce-scatter.2.cloned.1.call-update) | async-done | bytes 196624 | tf_op jit(solution)/shard_map/reduce_scatter | solution.py:49
Async XLA Ops:
  7.2 31.0 %all-gather.5.cloned.1.call-start = ((), (), s32[]{:S(2)}) async-start(), calls=%async_computation.3 | async-start | bytes 1769472 | tf_op jit(solution)/shard_map/all_gather | solution.py:26
  7.9 57.8 %all-gather.7.cloned.1.call-start = ((), (), s32[]{:S(2)}) async-start(), calls=%async_computation.4 | async-start | bytes 1769472 | tf_op jit(solution)/shard_map/all_gather | solution.py:25
  44.7 40.9 %all-to-all-start = ((bf16[4,128,1536]{2,1,0:T(8,128)(2,1)}), bf16[4,128,1536]{2,1,0:T(8,128)(2,1)S(1)}, u32[]{:S(2)}, u32[]{:S(2)}) async-start(bf16[4,128,1536]{2,1,0:T(8,128)(2,1)} %bitcast), calls=%async_computation | async-start | bytes 3145728 | tf_op jit(solution)/shard_map/all_to_all | solution.py:40
  85.6 40.0 %all-to-all-start.1 = ((bf16[4,128,1536]{2,1,0:T(8,128)(2,1)}), bf16[4,128,1536]{2,1,0:T(8,128)(2,1)S(1)}, u32[]{:S(2)}, u32[]{:S(2)}) async-start(bf16[4,128,1536]{2,1,0:T(8,128)(2,1)} %bitcast.14), calls=%async_computation.1 | async-start | bytes 3145728 | tf_op jit(solution)/shard_map/all_to_all | solution.py:39
  89.2 74.1 %all-gather.9.cloned.1.call-start = ((), (), s32[]{:S(2)}) async-start(), calls=%async_computation.5 | async-start | bytes 1966080 | tf_op jit(solution)/shard_map/all_gather | solution.py:47
  90.3 35.5 %copy-start = (f32[128,1536]{1,0:T(8,128)S(1)}, f32[128,1536]{1,0:T(8,128)}, u32[]{:S(2)}) copy-start(f32[128,1536]{1,0:T(8,128)} %convert_reduce_fusion.1) | copy-start | bytes 2359300
  127.2 73.5 %all-gather.11.cloned.1.call-start = ((), (), s32[]{:S(2)}) async-start(), calls=%async_computation.7 | async-start | bytes 1966080 | tf_op jit(solution)/shard_map/all_gather | solution.py:46
  127.8 114.1 %reduce-scatter.2.cloned.1.call-start = ((), (), s32[]{:S(2)}) async-start(), calls=%async_computation.6 | async-start | bytes 1769472 | tf_op jit(solution)/shard_map/reduce_scatter | solution.py:49
  163.3 6.8 %copy-start.3 = (bf16[512,1536]{1,0:T(8,128)(2,1)S(1)}, bf16[512,1536]{1,0:T(8,128)(2,1)}, u32[]{:S(2)}) copy-start(bf16[512,1536]{1,0:T(8,128)(2,1)} %all-gather.9.cloned.1.call-done) | copy-start | bytes 4718596
  170.0 1.5 copy-start.2
  175.8 24.9 %copy-start.1 = (bf16[512,1536]{1,0:T(8,128)(2,1)S(1)}, bf16[512,1536]{1,0:T(8,128)(2,1)}, u32[]{:S(2)}) copy-start(bf16[512,1536]{1,0:T(8,128)(2,1)} %all-gather.5.cloned.1.call-done) | copy-start | bytes 4718596
Sparse Core Ops, SparseCore 0:
  9.9 28.1 all-gather.4
  40.0 25.6 all-gather.6
  127.4 35.8 all-gather.8
  164.7 35.9 all-gather.10
  204.4 37.4 reduce-scatter.1
where the time goes:
time: 250 us; the launch traced here: 248 us
  waiting for transfers between devices  186 us (74%)
  matrix products  29.8 us (12%)
  between operations  13.8 us (6%)
  local copies, waits for them, and re-layouts  8.19 us (3%)
  starting transfers between devices  8.08 us (3%)
  other arithmetic  2.72 us (1%)
    reduce_scatter x1, waiting for transfers between devices, on_device(): lax.psum_scatter(lax.dot_general(slope_all, w_in, (((1,), (1,)), ((), ())...  35.5 us
    all_gather x1, waiting for transfers between devices, on_device(): lax.all_gather(slope_share, 'col', axis=0, tiled=True)  35.4 us
    all_to_all x1, waiting for transfers between devices, on_device(): lax.all_to_all(pre_blocks, 'col', split_axis=0, concat_axis=0, tiled=True)  35.3 us
    all_gather x1, waiting for transfers between devices, on_device(): lax.all_gather(cotangent, 'row', axis=0, tiled=True)  29.5 us
    all_gather x1, waiting for transfers between devices, on_device(): lax.all_gather(act_share, 'col', axis=0, tiled=True)  18.2 us
    all_gather x1, waiting for transfers between devices, on_device(): lax.all_gather(inputs, 'row', axis=0, tiled=True)  16.7 us
    all_to_all x1, waiting for transfers between devices, on_device(): lax.all_to_all(back_blocks, 'col', split_axis=0, concat_axis=0, tiled=True)  13.3 us
    unnamed x9, local copies, waits for them, and re-layouts  8.19 us
  transfers between devices with their start and end apart: 7, of which 7 were waited for; matrix products, arithmetic and copies ran while one was open for 15% of the time, Pallas kernels for 0%

commit v1 on v0

v1 whole, which is shorter than its diff:
```python
import functools
import math

import jax
import jax.numpy as jnp
from jax import lax
from jax.experimental import pallas as pl
from jax.experimental.pallas import tpu as pltpu
from jax.sharding import PartitionSpec as P

cubic_coef = 0.044715
tanh_scale = math.sqrt(2.0 / math.pi)
MESH = pl.DeviceIdType.MESH
NT = (((1,), (1,)), ((), ()))


def activate(pre, back):
    inner = tanh_scale * (pre + cubic_coef * pre * pre * pre)
    tval = jnp.tanh(inner)
    act = (0.5 * pre * (1.0 + tval)).astype(jnp.bfloat16)
    deriv = 0.5 * (1.0 + tval) + 0.5 * pre * (1.0 - tval * tval) * tanh_scale * (
        1.0 + 3.0 * cubic_coef * pre * pre
    )
    slope = (back * deriv).astype(jnp.bfloat16)
    return (act, slope)


def tile_of(width):
    for tile in (512, 384, 256, 128):
        if width % tile == 0:
            return tile
    return width


def kernel(
    rows, cols, own, in_ref, cot_ref, win_hbm, wout_hbm,
    gi_ref, whole_out, res_out,
    win, wout, whole, part, arrived, res, gpart, grecv,
    w_sem, ag_send, ag_recv, red_send, red_recv, bc_send, bc_recv, gi_send, gi_recv, out_sem,
):
    me = lax.axis_index("row")
    z = lax.axis_index("col")
    panel = 2 * own
    panels = rows // 2
    chip = me // 2
    feat = whole.shape[2]
    hidden = part.shape[2]
    last = cols - 1

    load_in = pltpu.make_async_copy(win_hbm, win, w_sem.at[0])
    load_out = pltpu.make_async_copy(wout_hbm, wout, w_sem.at[1])
    load_in.start()
    load_out.start()

    barrier = pltpu.get_barrier_semaphore()

    def greet(i, carry):
        other = lax.rem(me + i, rows)
        pl.semaphore_signal(barrier, inc=1, device_id={"row": other}, device_id_type=MESH)
        return carry

    lax.fori_loop(1, rows, greet, 0)

    @pl.when(z > 0)
    def _():
        pl.semaphore_signal(barrier, inc=1, device_id={"col": z - 1}, device_id_type=MESH)

    @pl.when(z < last)
    def _():
        pl.semaphore_signal(barrier, inc=1, device_id={"col": z + 1}, device_id_type=MESH)

    def block(row):
        return pl.ds(pl.multiple_of(row * own, own), own)

    whole[0, block(me), :] = in_ref[...]
    whole[1, block(me), :] = cot_ref[...]
    pl.semaphore_wait(barrier, rows - 1 + jnp.where(z > 0, 1, 0) + jnp.where(z < last, 1, 0))

    def gather_copy(src, dst):
        return pltpu.make_async_remote_copy(
            src_ref=whole.at[:, block(src), :],
            dst_ref=whole.at[:, block(src), :],
            send_sem=ag_send.at[dst],
            recv_sem=ag_recv.at[src],
            device_id={"row": dst},
            device_id_type=MESH,
        )

    sibling = me + 1 - 2 * lax.rem(me, 2)
    gather_copy(me, sibling).start()

    def push(j, carry):
        target = lax.rem(chip + panels - j, panels)
        gather_copy(me, 2 * target).start()
        gather_copy(me, 2 * target + 1).start()
        return carry

    lax.fori_loop(1, panels, push, 0)

    def panel_of(step):
        return lax.rem(chip + step, panels)

    def half(k, side):
        return block(2 * k + side)

    def red_copy(k, side, target):
        return pltpu.make_async_remote_copy(
            src_ref=part.at[:, half(k, side), :],
            dst_ref=arrived.at[:, half(k, side), :],
            send_sem=red_send.at[side, k],
            recv_sem=red_recv.at[side, k],
            device_id={"col": target},
            device_id_type=MESH,
        )

    def bc_copy(k, side, target):
        return pltpu.make_async_remote_copy(
            src_ref=res.at[:, half(k, side), :],
            dst_ref=res.at[:, half(k, side), :],
            send_sem=bc_send.at[side, k],
            recv_sem=bc_recv.at[side, k],
            device_id={"col": target},
            device_id_type=MESH,
        )

    def gi_copy(owner, src):
        return pltpu.make_async_remote_copy(
            src_ref=gpart.at[block(owner), :],
            dst_ref=grecv.at[src],
            send_sem=gi_send.at[owner],
            recv_sem=gi_recv.at[src],
            device_id={"row": owner},
            device_id_type=MESH,
        )

    place = (z, last - z)
    onward = (1, -1)
    lag = jnp.maximum(z, last - z)

    def forward(step):
        k = panel_of(step)

        @pl.when(step == 0)
        def _():
            gather_copy(sibling, sibling).wait_recv()
            load_in.wait()
            load_out.wait()

        @pl.when(step > 0)
        def _():
            gather_copy(2 * k, sibling).wait_recv()
            gather_copy(2 * k + 1, sibling).wait_recv()

        these = pl.ds(pl.multiple_of(k * panel, panel), panel)
        tile = tile_of(hidden)

        def one(c, carry):
            lanes = pl.ds(pl.multiple_of(c * tile, tile), tile)
            part[0, these, lanes] = jnp.dot(
                whole[0, these, :], win[:, lanes], preferred_element_type=jnp.float32
            ).astype(jnp.bfloat16)
            part[1, these, lanes] = lax.dot_general(
                whole[1, these, :], wout[lanes, :], NT, preferred_element_type=jnp.float32
            ).astype(jnp.bfloat16)
            return carry

        lax.fori_loop(0, hidden // tile, one, 0)

    def reduce_half(step, side):
        k = panel_of(step)
        p = place[side]

        @pl.when(p > 0)
        def _():
            red_copy(k, side, z).wait_recv()

        def summed(which, lines):
            return part[which, lines, :].astype(jnp.float32) + arrived[which, lines, :].astype(jnp.float32)

        def piece(i):
            return pl.ds(pl.multiple_of((2 * k + side) * own + i * 16, 16), 16)

        @pl.when(jnp.logical_and(p > 0, p < last))
        def _():
            def add(i, carry):
                lines = piece(i)
                part[0, lines, :] = summed(0, lines).astype(jnp.bfloat16)
                part[1, lines, :] = summed(1, lines).astype(jnp.bfloat16)
                return carry

            lax.fori_loop(0, own // 16, add, 0)

        @pl.when(p < last)
        def _():
            red_copy(k, side, z + onward[side]).start()

        @pl.when(p == last)
        def _():
            def finish(i, carry):
                lines = piece(i)
                act, slope = activate(summed(0, lines), summed(1, lines))
                res[0, lines, :] = act
                res[1, lines, :] = slope
                return carry

            lax.fori_loop(0, own // 16, finish, 0)
            bc_copy(k, side, z - onward[side]).start()

    def spread_half(step, side):
        k = panel_of(step)
        p = place[side]
        bc_copy(k, side, z).wait_recv()

        @pl.when(p > 0)
        def _():
            bc_copy(k, side, z - onward[side]).start()

    def backward(step):
        k = panel_of(step)
        these = pl.ds(pl.multiple_of(k * panel, panel), panel)
        tile = tile_of(feat)

        def one(c, carry):
            lanes = pl.ds(pl.multiple_of(c * tile, tile), tile)
            gpart[these, lanes] = lax.dot_general(
                res[1, these, :], win[lanes, :], NT, preferred_element_type=jnp.float32
            ).astype(jnp.bfloat16)
            return carry

        lax.fori_loop(0, feat // tile, one, 0)
        for side in range(2):
            owner = 2 * k + side

            @pl.when(owner != me)
            def _():
                gi_copy(owner, me).start()

    def tick(t, carry):
        @pl.when(t < panels)
        def _():
            forward(t)

        back_step = t - 1 - last - lag

        @pl.when(jnp.logical_and(back_step >= 0, back_step < panels))
        def _():
            backward(back_step)

        for side in range(2):
            step = t - place[side]

            @pl.when(jnp.logical_and(step >= 0, step < panels))
            def _():
                reduce_half(step, side)

        for side in range(2):
            step = t - last - (last - place[side])

            @pl.when(jnp.logical_and(place[side] < last, jnp.logical_and(step >= 0, step < panels)))
            def _():
                spread_half(step, side)

        return carry

    lax.fori_loop(0, panels + 2 * last + 1, tick, 0)

    out_whole = pltpu.make_async_copy(whole, whole_out, out_sem.at[0])
    out_res = pltpu.make_async_copy(res, res_out, out_sem.at[1])
    out_whole.start()
    out_res.start()

    def arrive(i, carry):
        src = lax.rem(me + i, rows)
        gi_copy(me, src).wait_recv()
        return carry

    lax.fori_loop(1, rows, arrive, 0)
    grecv[me] = gpart[block(me), :]

    def total(i, carry):
        lines = pl.ds(pl.multiple_of(i * 16, 16), 16)
        acc = grecv[0, lines, :].astype(jnp.float32)
        for r in range(1, rows):
            acc = acc + grecv[r, lines, :].astype(jnp.float32)
        gi_ref[lines, :] = acc.astype(jnp.bfloat16)
        return carry

    lax.fori_loop(0, own // 16, total, 0)

    def drain(i, carry):
        other = lax.rem(me + i, rows)
        gather_copy(me, other).wait_send()
        gi_copy(other, me).wait_send()
        return carry

    lax.fori_loop(1, rows, drain, 0)

    def drain_chain(k, carry):
        for side in range(2):
            @pl.when(place[side] < last)
            def _():
                red_copy(k, side, z).wait_send()

            @pl.when(place[side] > 0)
            def _():
                bc_copy(k, side, z).wait_send()

        return carry

    lax.fori_loop(0, panels, drain_chain, 0)
    out_whole.wait()
    out_res.wait()


def on_device(rows, cols, inputs, cotangent, w_in, w_out):
    own, feat = inputs.shape
    hidden = w_in.shape[1]
    tokens = own * rows
    bf16 = jnp.bfloat16
    vmem = pl.BlockSpec(memory_space=pltpu.VMEM)
    anywhere = pl.BlockSpec(memory_space=pl.ANY)
    dma = pltpu.SemaphoreType.DMA
    panels = rows // 2
    grad_inputs, whole, res = pl.pallas_call(
        functools.partial(kernel, rows, cols, own),
        out_shape=(
            jax.ShapeDtypeStruct((own, feat), bf16),
            jax.ShapeDtypeStruct((2, tokens, feat), bf16),
            jax.ShapeDtypeStruct((2, tokens, hidden), bf16),
        ),
        in_specs=[vmem, vmem, anywhere, anywhere],
        out_specs=(vmem, anywhere, anywhere),
        scratch_shapes=[
            pltpu.VMEM((feat, hidden), bf16),
            pltpu.VMEM((hidden, feat), bf16),
            pltpu.VMEM((2, tokens, feat), bf16),
            pltpu.VMEM((2, tokens, hidden), bf16),
            pltpu.VMEM((2, tokens, hidden), bf16),
            pltpu.VMEM((2, tokens, hidden), bf16),
            pltpu.VMEM((tokens, feat), bf16),
            pltpu.VMEM((rows, own, feat), bf16),
            dma((2,)),
            dma((rows,)),
            dma((rows,)),
            dma((2, panels)),
            dma((2, panels)),
            dma((2, panels)),
            dma((2, panels)),
            dma((rows,)),
            dma((rows,)),
            dma((2,)),
        ],
        compiler_params=pltpu.CompilerParams(
            collective_id=0, has_side_effects=True, vmem_limit_bytes=48 * 1024 * 1024
        ),
        name="mlp_backward",
    )(inputs, cotangent, w_in, w_out)
    grad_w_in = lax.dot_general(
        whole[0], res[1], (((0,), (0,)), ((), ())), preferred_element_type=jnp.float32
    ).astype(bf16)
    grad_w_out = lax.dot_general(
        res[0], whole[1], (((0,), (0,)), ((), ())), preferred_element_type=jnp.float32
    ).astype(bf16)
    return (grad_inputs, grad_w_in, grad_w_out)


def solution(mesh):
    return jax.shard_map(
        functools.partial(on_device, mesh.shape["row"], mesh.shape["col"]),
        mesh=mesh,
        in_specs=(P("row", "col"), P("row", "col"), P("col", "row"), P("row", "col")),
        out_specs=(P("row", "col"), P("col", "row"), P("row", "col")),
        check_vma=False,
    )
```

time: 250 us -> 138 us (0.55)
  waiting for transfers between devices: 186 us -> 0 us
  Pallas kernels: 0 us -> 124 us
  matrix products: 29.8 us -> 10.1 us
  between operations: 13.8 us -> 0.66 us
  starting transfers between devices: 8.08 us -> 0 us
  local copies, waits for them, and re-layouts: 8.19 us -> 2.53 us
  other arithmetic: 2.72 us -> 0 us
    pallas_call x0 -> x1, Pallas kernels: none -> 124 us  [on_device(): pl.pallas_call(functools.partial(kernel, rows, cols, own), out_shape=(jax...]
    all_gather x4 -> x0, waiting for transfers between devices: 99.8 us -> none  [the longest x1 35.4 us: on_device(): lax.all_gather(slope_share, 'col', axis=0, tiled=True)]
    all_to_all x2 -> x0, waiting for transfers between devices: 48.6 us -> none  [the longest x1 35.3 us: on_device(): lax.all_to_all(pre_blocks, 'col', split_axis=0, concat_axis=0, tiled=True)]
    reduce_scatter x1 -> x0, waiting for transfers between devices: 35.5 us -> none  [on_device(): lax.psum_scatter(lax.dot_general(slope_all, w_in, (((1,), (1,)), ((), ())...]
    dot_general x5 -> x2, matrix products: 29.8 us -> 10.1 us  [the longest x1 5.85 us: on_device(): lax.dot_general(res[0], whole[1], (((0,), (0,)), ((), ())), preferred_ele...]
    all_to_all x2 -> x0, starting transfers between devices: 7.88 us -> none  [the longest x1 4.32 us: on_device(): lax.all_to_all(back_blocks, 'col', split_axis=0, concat_axis=0, tiled=True)]
    unnamed x9 -> x7, local copies, waits for them, and re-layouts: 8.19 us -> 2.53 us
  transfers between devices with their start and end apart: 7 -> 0, of which waited for: 7 -> 0; matrix products, arithmetic and copies ran while one was open for 15% -> 0% of each run, Pallas kernels for 0% -> 0%
where the time goes in v1:
time: 138 us; the launch traced here: 137 us
  Pallas kernels  124 us (90%)
  matrix products  10.1 us (7%)
  local copies, waits for them, and re-layouts  2.53 us (2%)
    pallas_call x1, Pallas kernels, on_device(): pl.pallas_call(functools.partial(kernel, rows, cols, own), out_shape=(jax...  124 us
    dot_general x1, matrix products, on_device(): lax.dot_general(res[0], whole[1], (((0,), (0,)), ((), ())), preferred_ele...  5.85 us
    dot_general x1, matrix products, on_device(): lax.dot_general(whole[0], res[1], (((0,), (0,)), ((), ())), preferred_ele...  4.27 us

profile of v1, /device:TPU:1, one launch (start us, length us, event | category | flops | bytes accessed | tf_op | source)
XLA Modules:
  0.0 137.4 jit_solution(14319612166675586657)
XLA Ops:
  0.6 0.0 copy-start
  0.6 0.9 copy-done
  1.6 0.0 copy-start.1
  1.6 0.9 copy-done.1
  2.5 124.1 %mlp_backward.1 = (bf16[64,1536]{1,0:T(8,128)(2,1)S(1)}, bf16[2,512,1536]{2,1,0:T(8,128)(2,1)S(1)}, bf16[2,512,1536]{2,1,0:T(8,128)(2,1)}) custom-call(bf16[64,1536]{1,0:T(8,128)(2,1)S(1)} %copy-done, bf16[64,1536]{1,0:T(8,128)(2,1)S(1)} %copy-done.1, bf16[1536,1536]{1,0:T(8,128)(2,1)} %win_hbm.1, bf16[1536,1536]{1,0:T(8,128)(2,1)} %wout_hbm.1), custom_call_target="tpu_custom_call" | custom-call | tf_op jit(solution)/shard_map/mlp_backward/pallas_call | solution.py:324
  126.6 0.0 copy-start.2
  126.6 5.9 %convolution_convert_fusion = bf16[1536,1536]{1,0:T(8,128)(2,1)} fusion(bf16[2,512,1536]{2,1,0:T(8,128)(2,1)S(1)} %get-tuple-element.7, bf16[2,512,1536]{2,1,0:T(8,128)(2,1)} %get-tuple-element.8), kind=kOutput, calls=%fused_computation | convolution fusion | flops 2418278400 | bytes 7864320 | tf_op jit(solution)/shard_map/dot_general | solution.py:361
  132.5 0.0 copy-done.2
  132.5 4.3 %convolution_convert_fusion.1 = bf16[1536,1536]{1,0:T(8,128)(2,1)} fusion(bf16[2,512,1536]{2,1,0:T(8,128)(2,1)S(1)} %copy-done.2, bf16[2,512,1536]{2,1,0:T(8,128)(2,1)S(1)} %get-tuple-element.7), kind=kOutput, calls=%fused_computation.1 | convolution fusion | flops 2418278400 | bytes 7864320 | tf_op jit(solution)/shard_map/dot_general | solution.py:358
  136.7 0.7 copy.8
Async XLA Ops:
  0.6 0.9 copy-start
  1.6 0.9 copy-start.1
  126.6 5.9 %copy-start.2 = (bf16[2,512,1536]{2,1,0:T(8,128)(2,1)S(1)}, bf16[2,512,1536]{2,1,0:T(8,128)(2,1)}, u32[]{:S(2)}) copy-start(bf16[2,512,1536]{2,1,0:T(8,128)(2,1)} %get-tuple-element.8) | copy-start | bytes 9437188

commit v2 on v1

--- a/solution.py
+++ b/solution.py
@@ -11,6 +11,7 @@
 cubic_coef = 0.044715
 tanh_scale = math.sqrt(2.0 / math.pi)
 MESH = pl.DeviceIdType.MESH
+SPLIT = 3
 NT = (((1,), (1,)), ((), ()))
 
 
@@ -33,9 +34,9 @@
 
 
 def kernel(
-    rows, cols, own, in_ref, cot_ref, win_hbm, wout_hbm,
+    rows, cols, own, split, in_ref, cot_ref, win_hbm, wout_hbm,
     gi_ref, whole_out, res_out,
-    win, wout, whole, part, arrived, res, gpart, grecv,
+    win, wout, whole, part, arrived, res, gpart, grecv, gacc,
     w_sem, ag_send, ag_recv, red_send, red_recv, bc_send, bc_recv, gi_send, gi_recv, out_sem,
 ):
     me = lax.axis_index("row")
@@ -46,11 +47,11 @@
     feat = whole.shape[2]
     hidden = part.shape[2]
     last = cols - 1
+    width = hidden // split
+    steps = panels * split
 
     load_in = pltpu.make_async_copy(win_hbm, win, w_sem.at[0])
     load_out = pltpu.make_async_copy(wout_hbm, wout, w_sem.at[1])
-    load_in.start()
-    load_out.start()
 
     barrier = pltpu.get_barrier_semaphore()
 
@@ -72,8 +73,14 @@
     def block(row):
         return pl.ds(pl.multiple_of(row * own, own), own)
 
-    whole[0, block(me), :] = in_ref[...]
-    whole[1, block(me), :] = cot_ref[...]
+    mine_in = pltpu.make_async_copy(in_ref, whole.at[0, block(me), :], w_sem.at[2])
+    mine_cot = pltpu.make_async_copy(cot_ref, whole.at[1, block(me), :], w_sem.at[3])
+    mine_in.start()
+    mine_cot.start()
+    load_in.start()
+    load_out.start()
+    mine_in.wait()
+    mine_cot.wait()
     pl.semaphore_wait(barrier, rows - 1 + jnp.where(z > 0, 1, 0) + jnp.where(z < last, 1, 0))
 
     def gather_copy(src, dst):
@@ -98,27 +105,33 @@
     lax.fori_loop(1, panels, push, 0)
 
     def panel_of(step):
-        return lax.rem(chip + step, panels)
+        return lax.rem(chip + step // split, panels)
+
+    def piece_of(step):
+        return lax.rem(step, split)
+
+    def lanes_of(h):
+        return pl.ds(pl.multiple_of(h * width, width), width)
 
     def half(k, side):
         return block(2 * k + side)
 
-    def red_copy(k, side, target):
+    def red_copy(k, h, side, target):
         return pltpu.make_async_remote_copy(
-            src_ref=part.at[:, half(k, side), :],
-            dst_ref=arrived.at[:, half(k, side), :],
-            send_sem=red_send.at[side, k],
-            recv_sem=red_recv.at[side, k],
+            src_ref=part.at[:, half(k, side), lanes_of(h)],
+            dst_ref=arrived.at[:, half(k, side), lanes_of(h)],
+            send_sem=red_send.at[side, k * split + h],
+            recv_sem=red_recv.at[side, k * split + h],
             device_id={"col": target},
             device_id_type=MESH,
         )
 
-    def bc_copy(k, side, target):
+    def bc_copy(k, h, side, target):
         return pltpu.make_async_remote_copy(
-            src_ref=res.at[:, half(k, side), :],
-            dst_ref=res.at[:, half(k, side), :],
-            send_sem=bc_send.at[side, k],
-            recv_sem=bc_recv.at[side, k],
+            src_ref=res.at[:, half(k, side), lanes_of(h)],
+            dst_ref=res.at[:, half(k, side), lanes_of(h)],
+            send_sem=bc_send.at[side, k * split + h],
+            recv_sem=bc_recv.at[side, k * split + h],
             device_id={"col": target},
             device_id_type=MESH,
         )
@@ -139,6 +152,7 @@
 
     def forward(step):
         k = panel_of(step)
+        h = piece_of(step)
 
         @pl.when(step == 0)
         def _():
@@ -146,16 +160,16 @@
             load_in.wait()
             load_out.wait()
 
-        @pl.when(step > 0)
+        @pl.when(jnp.logical_and(step > 0, h == 0))
         def _():
             gather_copy(2 * k, sibling).wait_recv()
             gather_copy(2 * k + 1, sibling).wait_recv()
 
         these = pl.ds(pl.multiple_of(k * panel, panel), panel)
-        tile = tile_of(hidden)
+        tile = tile_of(width)
 
         def one(c, carry):
-            lanes = pl.ds(pl.multiple_of(c * tile, tile), tile)
+            lanes = pl.ds(pl.multiple_of(h * width + c * tile, tile), tile)
             part[0, these, lanes] = jnp.dot(
                 whole[0, these, :], win[:, lanes], preferred_element_type=jnp.float32
             ).astype(jnp.bfloat16)
@@ -164,18 +178,20 @@
             ).astype(jnp.bfloat16)
             return carry
 
-        lax.fori_loop(0, hidden // tile, one, 0)
+        lax.fori_loop(0, width // tile, one, 0)
 
     def reduce_half(step, side):
         k = panel_of(step)
+        h = piece_of(step)
+        lanes = lanes_of(h)
         p = place[side]
 
         @pl.when(p > 0)
         def _():
-            red_copy(k, side, z).wait_recv()
+            red_copy(k, h, side, z).wait_recv()
 
         def summed(which, lines):
-            return part[which, lines, :].astype(jnp.float32) + arrived[which, lines, :].astype(jnp.float32)
+            return part[which, lines, lanes].astype(jnp.float32) + arrived[which, lines, lanes].astype(jnp.float32)
 
         def piece(i):
             return pl.ds(pl.multiple_of((2 * k + side) * own + i * 16, 16), 16)
@@ -184,85 +200,104 @@
         def _():
             def add(i, carry):
                 lines = piece(i)
-                part[0, lines, :] = summed(0, lines).astype(jnp.bfloat16)
-                part[1, lines, :] = summed(1, lines).astype(jnp.bfloat16)
+                part[0, lines, lanes] = summed(0, lines).astype(jnp.bfloat16)
+                part[1, lines, lanes] = summed(1, lines).astype(jnp.bfloat16)
                 return carry
 
             lax.fori_loop(0, own // 16, add, 0)
 
         @pl.when(p < last)
         def _():
-            red_copy(k, side, z + onward[side]).start()
+            red_copy(k, h, side, z + onward[side]).start()
 
         @pl.when(p == last)
         def _():
             def finish(i, carry):
                 lines = piece(i)
                 act, slope = activate(summed(0, lines), summed(1, lines))
-                res[0, lines, :] = act
-                res[1, lines, :] = slope
+                res[0, lines, lanes] = act
+                res[1, lines, lanes] = slope
                 return carry
 
             lax.fori_loop(0, own // 16, finish, 0)
-            bc_copy(k, side, z - onward[side]).start()
+            bc_copy(k, h, side, z - onward[side]).start()
 
     def spread_half(step, side):
         k = panel_of(step)
+        h = piece_of(step)
         p = place[side]
-        bc_copy(k, side, z).wait_recv()
+        bc_copy(k, h, side, z).wait_recv()
 
         @pl.when(p > 0)
         def _():
-            bc_copy(k, side, z - onward[side]).start()
+            bc_copy(k, h, side, z - onward[side]).start()
 
     def backward(step):
         k = panel_of(step)
+        h = piece_of(step)
         these = pl.ds(pl.multiple_of(k * panel, panel), panel)
         tile = tile_of(feat)
 
         def one(c, carry):
             lanes = pl.ds(pl.multiple_of(c * tile, tile), tile)
-            gpart[these, lanes] = lax.dot_general(
-                res[1, these, :], win[lanes, :], NT, preferred_element_type=jnp.float32
-            ).astype(jnp.bfloat16)
+            term = lax.dot_general(
+                res[1, these, lanes_of(h)],
+                win[lanes, lanes_of(h)],
+                NT,
+                preferred_element_type=jnp.float32,
+            )
+            if split > 1:
+                @pl.when(h == 0)
+                def _():
+                    gacc[:, lanes] = term
+
+                @pl.when(h > 0)
+                def _():
+                    gacc[:, lanes] += term
+
+                @pl.when(h == split - 1)
+                def _():
+                    gpart[these, lanes] = gacc[:, lanes].astype(jnp.bfloat16)
+            else:
+                gpart[these, lanes] = term.astype(jnp.bfloat16)
             return carry
 
         lax.fori_loop(0, feat // tile, one, 0)
         for side in range(2):
             owner = 2 * k + side
 
-            @pl.when(owner != me)
+            @pl.when(jnp.logical_and(owner != me, h == split - 1))
             def _():
                 gi_copy(owner, me).start()
 
     def tick(t, carry):
-        @pl.when(t < panels)
+        @pl.when(t < steps)
         def _():
             forward(t)
 
         back_step = t - 1 - last - lag
 
-        @pl.when(jnp.logical_and(back_step >= 0, back_step < panels))
+        @pl.when(jnp.logical_and(back_step >= 0, back_step < steps))
         def _():
             backward(back_step)
 
         for side in range(2):
             step = t - place[side]
 
-            @pl.when(jnp.logical_and(step >= 0, step < panels))
+            @pl.when(jnp.logical_and(step >= 0, step < steps))
             def _():
                 reduce_half(step, side)
 
         for side in range(2):
             step = t - last - (last - place[side])
 
-            @pl.when(jnp.logical_and(place[side] < last, jnp.logical_and(step >= 0, step < panels)))
+            @pl.when(jnp.logical_and(place[side] < last, jnp.logical_and(step >= 0, step < steps)))
             def _():
                 spread_half(step, side)
 
         return carry
 
-    lax.fori_loop(0, panels + 2 * last + 1, tick, 0)
+    lax.fori_loop(0, steps + 2 * last + 1, tick, 0)
 
     out_whole = pltpu.make_async_copy(whole, whole_out, out_sem.at[0])
     out_res = pltpu.make_async_copy(res, res_out, out_sem.at[1])
@@ -295,19 +330,21 @@
 
     lax.fori_loop(1, rows, drain, 0)
 
-    def drain_chain(k, carry):
+    def drain_chain(step, carry):
+        k = step // split
+        h = piece_of(step)
         for side in range(2):
             @pl.when(place[side] < last)
             def _():
-                red_copy(k, side, z).wait_send()
+                red_copy(k, h, side, z).wait_send()
 
             @pl.when(place[side] > 0)
             def _():
-                bc_copy(k, side, z).wait_send()
-
-        return carry
-
-    lax.fori_loop(0, panels, drain_chain, 0)
+                bc_copy(k, h, side, z).wait_send()
+
+        return carry
+
+    lax.fori_loop(0, steps, drain_chain, 0)
     out_whole.wait()
     out_res.wait()
 
@@ -320,15 +357,16 @@
     vmem = pl.BlockSpec(memory_space=pltpu.VMEM)
     anywhere = pl.BlockSpec(memory_space=pl.ANY)
     dma = pltpu.SemaphoreType.DMA
-    panels = rows // 2
+    split = SPLIT if hidden % (128 * SPLIT) == 0 else 1
+    steps = rows // 2 * split
     grad_inputs, whole, res = pl.pallas_call(
-        functools.partial(kernel, rows, cols, own),
+        functools.partial(kernel, rows, cols, own, split),
         out_shape=(
             jax.ShapeDtypeStruct((own, feat), bf16),
             jax.ShapeDtypeStruct((2, tokens, feat), bf16),
             jax.ShapeDtypeStruct((2, tokens, hidden), bf16),
         ),
-        in_specs=[vmem, vmem, anywhere, anywhere],
+        in_specs=[anywhere] * 4,
         out_specs=(vmem, anywhere, anywhere),
         scratch_shapes=[
             pltpu.VMEM((feat, hidden), bf16),
@@ -339,13 +377,14 @@
             pltpu.VMEM((2, tokens, hidden), bf16),
             pltpu.VMEM((tokens, feat), bf16),
             pltpu.VMEM((rows, own, feat), bf16),
-            dma((2,)),
+            pltpu.VMEM((2 * own, feat), jnp.float32),
+            dma((4,)),
             dma((rows,)),
             dma((rows,)),
-            dma((2, panels)),
-            dma((2, panels)),
-            dma((2, panels)),
-            dma((2, panels)),
+            dma((2, steps)),
+            dma((2, steps)),
+            dma((2, steps)),
+            dma((2, steps)),
             dma((rows,)),
             dma((rows,)),
             dma((2,)),

time: 138 us -> 121 us (0.88)
  Pallas kernels: 124 us -> 108 us
    pallas_call x1, Pallas kernels: 124 us -> 108 us  [on_device(): pl.pallas_call(functools.partial(kernel, rows, cols, own, split), out_sha...]
where the time goes in v2:
time: 121 us
  Pallas kernels  108 us (89%)
  matrix products  10.1 us (8%)
  local copies, waits for them, and re-layouts  2.53 us (2%)
    pallas_call x1, Pallas kernels, on_device(): pl.pallas_call(functools.partial(kernel, rows, cols, own, split), out_sha...  108 us
    dot_general x1, matrix products, on_device(): lax.dot_general(res[0], whole[1], (((0,), (0,)), ((), ())), preferred_ele...  5.85 us
    dot_general x1, matrix products, on_device(): lax.dot_general(whole[0], res[1], (((0,), (0,)), ((), ())), preferred_ele...  4.27 us
    unnamed x7, local copies, waits for them, and re-layouts  2.53 us

profile of v2, /device:TPU:1, one launch (start us, length us, event | category | flops | bytes accessed | tf_op | source)
XLA Modules:
  0.0 120.8 jit_solution(1055267258603564555)
XLA Ops:
  0.6 0.0 copy-start
  0.6 0.9 copy-done
  1.6 0.0 copy-start.1
  1.6 0.9 copy-done.1
  2.5 107.5 %mlp_backward.1 = (bf16[64,1536]{1,0:T(8,128)(2,1)S(1)}, bf16[2,512,1536]{2,1,0:T(8,128)(2,1)S(1)}, bf16[2,512,1536]{2,1,0:T(8,128)(2,1)}) custom-call(bf16[64,1536]{1,0:T(8,128)(2,1)S(1)} %copy-done, bf16[64,1536]{1,0:T(8,128)(2,1)S(1)} %copy-done.1, bf16[1536,1536]{1,0:T(8,128)(2,1)} %win_hbm.1, bf16[1536,1536]{1,0:T(8,128)(2,1)} %wout_hbm.1), custom_call_target="tpu_custom_call" | custom-call | tf_op jit(solution)/shard_map/mlp_backward/pallas_call | solution.py:362
  110.0 0.0 copy-start.2
  110.0 5.9 %convolution_convert_fusion = bf16[1536,1536]{1,0:T(8,128)(2,1)} fusion(bf16[2,512,1536]{2,1,0:T(8,128)(2,1)S(1)} %get-tuple-element.7, bf16[2,512,1536]{2,1,0:T(8,128)(2,1)} %get-tuple-element.8), kind=kOutput, calls=%fused_computation | convolution fusion | flops 2418278400 | bytes 7864320 | tf_op jit(solution)/shard_map/dot_general | solution.py:400
  115.9 0.0 copy-done.2
  115.9 4.3 %convolution_convert_fusion.1 = bf16[1536,1536]{1,0:T(8,128)(2,1)} fusion(bf16[2,512,1536]{2,1,0:T(8,128)(2,1)S(1)} %copy-done.2, bf16[2,512,1536]{2,1,0:T(8,128)(2,1)S(1)} %get-tuple-element.7), kind=kOutput, calls=%fused_computation.1 | convolution fusion | flops 2418278400 | bytes 7864320 | tf_op jit(solution)/shard_map/dot_general | solution.py:397
  120.1 0.7 copy.8
Async XLA Ops:
  0.6 0.9 copy-start
  1.6 0.9 copy-start.1
  110.0 5.9 %copy-start.2 = (bf16[2,512,1536]{2,1,0:T(8,128)(2,1)S(1)}, bf16[2,512,1536]{2,1,0:T(8,128)(2,1)}, u32[]{:S(2)}) copy-start(bf16[2,512,1536]{2,1,0:T(8,128)(2,1)} %get-tuple-element.8) | copy-start | bytes 9437188

commit v3 on v2

--- a/solution.py
+++ b/solution.py
@@ -11,7 +11,8 @@
 cubic_coef = 0.044715
 tanh_scale = math.sqrt(2.0 / math.pi)
 MESH = pl.DeviceIdType.MESH
-SPLIT = 3
+SPLIT = 6
+SKEW = 2
 NT = (((1,), (1,)), ((), ()))
 
 
@@ -275,21 +276,21 @@
         def _():
             forward(t)
 
-        back_step = t - 1 - last - lag
+        back_step = t - 1 - SKEW * (last + lag)
 
         @pl.when(jnp.logical_and(back_step >= 0, back_step < steps))
         def _():
             backward(back_step)
 
         for side in range(2):
-            step = t - place[side]
+            step = t - SKEW * place[side]
 
             @pl.when(jnp.logical_and(step >= 0, step < steps))
             def _():
                 reduce_half(step, side)
 
         for side in range(2):
-            step = t - last - (last - place[side])
+            step = t - SKEW * (2 * last - place[side])
 
             @pl.when(jnp.logical_and(place[side] < last, jnp.logical_and(step >= 0, step < steps)))
             def _():
@@ -297,7 +298,7 @@
 
         return carry
 
-    lax.fori_loop(0, steps + 2 * last + 1, tick, 0)
+    lax.fori_loop(0, steps + 2 * SKEW * last + 1, tick, 0)
 
     out_whole = pltpu.make_async_copy(whole, whole_out, out_sem.at[0])
     out_res = pltpu.make_async_copy(res, res_out, out_sem.at[1])
@@ -390,7 +391,7 @@
             dma((2,)),
         ],
         compiler_params=pltpu.CompilerParams(
-            collective_id=0, has_side_effects=True, vmem_limit_bytes=48 * 1024 * 1024
+            collective_id=0, has_side_effects=True, vmem_limit_bytes=60 * 1024 * 1024
         ),
         name="mlp_backward",
     )(inputs, cotangent, w_in, w_out)

time: 121 us -> 117 us (0.967)
  Pallas kernels: 108 us -> 104 us
  local copies, waits for them, and re-layouts: 2.53 us -> 0.69 us
    pallas_call x1, Pallas kernels: 108 us -> 104 us  [on_device(): pl.pallas_call(functools.partial(kernel, rows, cols, own, split), out_sha...]
    unnamed x7, local copies, waits for them, and re-layouts: 2.53 us -> 0.69 us
where the time goes in v3:
time: 117 us
  Pallas kernels  104 us (89%)
  matrix products  11.2 us (10%)
    pallas_call x1, Pallas kernels, on_device(): pl.pallas_call(functools.partial(kernel, rows, cols, own, split), out_sha...  104 us
    dot_general x1, matrix products, on_device(): lax.dot_general(res[0], whole[1], (((0,), (0,)), ((), ())), preferred_ele...  6.87 us
    dot_general x1, matrix products, on_device(): lax.dot_general(whole[0], res[1], (((0,), (0,)), ((), ())), preferred_ele...  4.31 us

profile of v3, /device:TPU:1, one launch (start us, length us, event | category | flops | bytes accessed | tf_op | source)
XLA Modules:
  0.0 116.6 jit_solution(2116618555110732396)
XLA Ops:
  0.6 104.1 %mlp_backward.1 = (bf16[64,1536]{1,0:T(8,128)(2,1)}, bf16[2,512,1536]{2,1,0:T(8,128)(2,1)}, bf16[2,512,1536]{2,1,0:T(8,128)(2,1)}) custom-call(bf16[64,1536]{1,0:T(8,128)(2,1)} %in_ref.1, bf16[64,1536]{1,0:T(8,128)(2,1)} %cot_ref.1, bf16[1536,1536]{1,0:T(8,128)(2,1)} %win_hbm.1, bf16[1536,1536]{1,0:T(8,128)(2,1)} %wout_hbm.1), custom_call_target="tpu_custom_call" | custom-call | tf_op jit(solution)/shard_map/mlp_backward/pallas_call | solution.py:363
  104.7 0.0 copy-start.1
  104.7 0.0 copy-start.2
  104.8 6.9 %convolution_convert_fusion = bf16[1536,1536]{1,0:T(8,128)(2,1)} fusion(bf16[2,512,1536]{2,1,0:T(8,128)(2,1)} %get-tuple-element.7, bf16[2,512,1536]{2,1,0:T(8,128)(2,1)} %get-tuple-element.8), kind=kOutput, calls=%fused_computation | convolution fusion | flops 2418278400 | bytes 7864320 | tf_op jit(solution)/shard_map/dot_general | solution.py:401
  111.6 0.0 copy-done.1
  111.6 0.0 copy-done.2
  111.6 0.0 copy-start
  111.6 4.3 %convolution_convert_fusion.1 = bf16[1536,1536]{1,0:T(8,128)(2,1)} fusion(bf16[2,512,1536]{2,1,0:T(8,128)(2,1)S(1)} %copy-done.2, bf16[2,512,1536]{2,1,0:T(8,128)(2,1)S(1)} %copy-done.1), kind=kOutput, calls=%fused_computation.1 | convolution fusion | flops 2418278400 | bytes 7864320 | tf_op jit(solution)/shard_map/dot_general | solution.py:398
  115.9 0.0 copy-done
  115.9 0.7 copy.8
Async XLA Ops:
  104.7 6.9 %copy-start.1 = (bf16[2,512,1536]{2,1,0:T(8,128)(2,1)S(1)}, bf16[2,512,1536]{2,1,0:T(8,128)(2,1)}, u32[]{:S(2)}) copy-start(bf16[2,512,1536]{2,1,0:T(8,128)(2,1)} %get-tuple-element.7) | copy-start | bytes 9437188
  104.7 6.9 %copy-start.2 = (bf16[2,512,1536]{2,1,0:T(8,128)(2,1)S(1)}, bf16[2,512,1536]{2,1,0:T(8,128)(2,1)}, u32[]{:S(2)}) copy-start(bf16[2,512,1536]{2,1,0:T(8,128)(2,1)} %get-tuple-element.8) | copy-start | bytes 9437188
  111.6 4.3 %copy-start = (bf16[64,1536]{1,0:T(8,128)(2,1)S(1)}, bf16[64,1536]{1,0:T(8,128)(2,1)}, u32[]{:S(2)}) copy-start(bf16[64,1536]{1,0:T(8,128)(2,1)} %get-tuple-element.12) | copy-start | bytes 589828

commit v4 on v3

--- a/solution.py
+++ b/solution.py
@@ -276,12 +276,6 @@
         def _():
             forward(t)
 
-        back_step = t - 1 - SKEW * (last + lag)
-
-        @pl.when(jnp.logical_and(back_step >= 0, back_step < steps))
-        def _():
-            backward(back_step)
-
         for side in range(2):
             step = t - SKEW * place[side]
 
@@ -296,9 +290,15 @@
             def _():
                 spread_half(step, side)
 
-        return carry
-
-    lax.fori_loop(0, steps + 2 * SKEW * last + 1, tick, 0)
+        back_step = t - SKEW * (last + lag)
+
+        @pl.when(jnp.logical_and(back_step >= 0, back_step < steps))
+        def _():
+            backward(back_step)
+
+        return carry
+
+    lax.fori_loop(0, steps + 2 * SKEW * last, tick, 0)
 
     out_whole = pltpu.make_async_copy(whole, whole_out, out_sem.at[0])
     out_res = pltpu.make_async_copy(res, res_out, out_sem.at[1])

time: 117 us -> 116 us (level)
  no operation moved by 1% of the time
where the time goes in v4:
time: 116 us
  Pallas kernels  104 us (90%)
  matrix products  11.2 us (10%)
    pallas_call x1, Pallas kernels, on_device(): pl.pallas_call(functools.partial(kernel, rows, cols, own, split), out_sha...  104 us
    dot_general x1, matrix products, on_device(): lax.dot_general(res[0], whole[1], (((0,), (0,)), ((), ())), preferred_ele...  6.87 us
    dot_general x1, matrix products, on_device(): lax.dot_general(whole[0], res[1], (((0,), (0,)), ((), ())), preferred_ele...  4.31 us

profile of v4, /device:TPU:1, one launch (start us, length us, event | category | flops | bytes accessed | tf_op | source)
XLA Modules:
  0.0 116.2 jit_solution(802682821236085600)
XLA Ops:
  0.6 103.7 %mlp_backward.1 = (bf16[64,1536]{1,0:T(8,128)(2,1)}, bf16[2,512,1536]{2,1,0:T(8,128)(2,1)}, bf16[2,512,1536]{2,1,0:T(8,128)(2,1)}) custom-call(bf16[64,1536]{1,0:T(8,128)(2,1)} %in_ref.1, bf16[64,1536]{1,0:T(8,128)(2,1)} %cot_ref.1, bf16[1536,1536]{1,0:T(8,128)(2,1)} %win_hbm.1, bf16[1536,1536]{1,0:T(8,128)(2,1)} %wout_hbm.1), custom_call_target="tpu_custom_call" | custom-call | tf_op jit(solution)/shard_map/mlp_backward/pallas_call | solution.py:363
  104.3 0.0 copy-start.1
  104.4 0.0 copy-start.2
  104.4 6.9 %convolution_convert_fusion = bf16[1536,1536]{1,0:T(8,128)(2,1)} fusion(bf16[2,512,1536]{2,1,0:T(8,128)(2,1)} %get-tuple-element.7, bf16[2,512,1536]{2,1,0:T(8,128)(2,1)} %get-tuple-element.8), kind=kOutput, calls=%fused_computation | convolution fusion | flops 2418278400 | bytes 7864320 | tf_op jit(solution)/shard_map/dot_general | solution.py:401
  111.2 0.0 copy-done.1
  111.2 0.0 copy-done.2
  111.2 0.0 copy-start
  111.2 4.3 %convolution_convert_fusion.1 = bf16[1536,1536]{1,0:T(8,128)(2,1)} fusion(bf16[2,512,1536]{2,1,0:T(8,128)(2,1)S(1)} %copy-done.2, bf16[2,512,1536]{2,1,0:T(8,128)(2,1)S(1)} %copy-done.1), kind=kOutput, calls=%fused_computation.1 | convolution fusion | flops 2418278400 | bytes 7864320 | tf_op jit(solution)/shard_map/dot_general | solution.py:398
  115.6 0.0 copy-done
  115.6 0.7 copy.8
Async XLA Ops:
  104.3 6.9 %copy-start.1 = (bf16[2,512,1536]{2,1,0:T(8,128)(2,1)S(1)}, bf16[2,512,1536]{2,1,0:T(8,128)(2,1)}, u32[]{:S(2)}) copy-start(bf16[2,512,1536]{2,1,0:T(8,128)(2,1)} %get-tuple-element.7) | copy-start | bytes 9437188
  104.4 6.9 %copy-start.2 = (bf16[2,512,1536]{2,1,0:T(8,128)(2,1)S(1)}, bf16[2,512,1536]{2,1,0:T(8,128)(2,1)}, u32[]{:S(2)}) copy-start(bf16[2,512,1536]{2,1,0:T(8,128)(2,1)} %get-tuple-element.8) | copy-start | bytes 9437188
  111.2 4.3 %copy-start = (bf16[64,1536]{1,0:T(8,128)(2,1)S(1)}, bf16[64,1536]{1,0:T(8,128)(2,1)}, u32[]{:S(2)}) copy-start(bf16[64,1536]{1,0:T(8,128)(2,1)} %get-tuple-element.12) | copy-start | bytes 589828

commit v5 on v4

--- a/solution.py
+++ b/solution.py
@@ -284,13 +284,13 @@
                 reduce_half(step, side)
 
         for side in range(2):
-            step = t - SKEW * (2 * last - place[side])
+            step = t - SKEW * last - (last - place[side])
 
             @pl.when(jnp.logical_and(place[side] < last, jnp.logical_and(step >= 0, step < steps)))
             def _():
                 spread_half(step, side)
 
-        back_step = t - SKEW * (last + lag)
+        back_step = t - SKEW * last - lag
 
         @pl.when(jnp.logical_and(back_step >= 0, back_step < steps))
         def _():
@@ -298,7 +298,7 @@
 
         return carry
 
-    lax.fori_loop(0, steps + 2 * SKEW * last, tick, 0)
+    lax.fori_loop(0, steps + SKEW * last + last, tick, 0)
 
     out_whole = pltpu.make_async_copy(whole, whole_out, out_sem.at[0])
     out_res = pltpu.make_async_copy(res, res_out, out_sem.at[1])

time: 116 us -> 125 us (1.078)
  Pallas kernels: 104 us -> 113 us
    pallas_call x1, Pallas kernels: 104 us -> 113 us  [on_device(): pl.pallas_call(functools.partial(kernel, rows, cols, own, split), out_sha...]
where the time goes in v5:
time: 125 us
  Pallas kernels  113 us (90%)
  matrix products  11.2 us (9%)
    pallas_call x1, Pallas kernels, on_device(): pl.pallas_call(functools.partial(kernel, rows, cols, own, split), out_sha...  113 us
    dot_general x1, matrix products, on_device(): lax.dot_general(res[0], whole[1], (((0,), (0,)), ((), ())), preferred_ele...  6.87 us
    dot_general x1, matrix products, on_device(): lax.dot_general(whole[0], res[1], (((0,), (0,)), ((), ())), preferred_ele...  4.31 us

profile of v5, /device:TPU:1, one launch (start us, length us, event | category | flops | bytes accessed | tf_op | source)
XLA Modules:
  0.0 125.1 jit_solution(3132062189433882503)
XLA Ops:
  0.6 112.6 %mlp_backward.1 = (bf16[64,1536]{1,0:T(8,128)(2,1)}, bf16[2,512,1536]{2,1,0:T(8,128)(2,1)}, bf16[2,512,1536]{2,1,0:T(8,128)(2,1)}) custom-call(bf16[64,1536]{1,0:T(8,128)(2,1)} %in_ref.1, bf16[64,1536]{1,0:T(8,128)(2,1)} %cot_ref.1, bf16[1536,1536]{1,0:T(8,128)(2,1)} %win_hbm.1, bf16[1536,1536]{1,0:T(8,128)(2,1)} %wout_hbm.1), custom_call_target="tpu_custom_call" | custom-call | tf_op jit(solution)/shard_map/mlp_backward/pallas_call | solution.py:363
  113.2 0.0 copy-start.1
  113.2 0.0 copy-start.2
  113.3 6.9 %convolution_convert_fusion = bf16[1536,1536]{1,0:T(8,128)(2,1)} fusion(bf16[2,512,1536]{2,1,0:T(8,128)(2,1)} %get-tuple-element.7, bf16[2,512,1536]{2,1,0:T(8,128)(2,1)} %get-tuple-element.8), kind=kOutput, calls=%fused_computation | convolution fusion | flops 2418278400 | bytes 7864320 | tf_op jit(solution)/shard_map/dot_general | solution.py:401
  120.1 0.0 copy-done.1
  120.1 0.0 copy-done.2
  120.1 0.0 copy-start
  120.1 4.3 %convolution_convert_fusion.1 = bf16[1536,1536]{1,0:T(8,128)(2,1)} fusion(bf16[2,512,1536]{2,1,0:T(8,128)(2,1)S(1)} %copy-done.2, bf16[2,512,1536]{2,1,0:T(8,128)(2,1)S(1)} %copy-done.1), kind=kOutput, calls=%fused_computation.1 | convolution fusion | flops 2418278400 | bytes 7864320 | tf_op jit(solution)/shard_map/dot_general | solution.py:398
  124.4 0.0 copy-done
  124.4 0.7 copy.8
Async XLA Ops:
  113.2 6.9 %copy-start.1 = (bf16[2,512,1536]{2,1,0:T(8,128)(2,1)S(1)}, bf16[2,512,1536]{2,1,0:T(8,128)(2,1)}, u32[]{:S(2)}) copy-start(bf16[2,512,1536]{2,1,0:T(8,128)(2,1)} %get-tuple-element.7) | copy-start | bytes 9437188
  113.2 6.9 %copy-start.2 = (bf16[2,512,1536]{2,1,0:T(8,128)(2,1)S(1)}, bf16[2,512,1536]{2,1,0:T(8,128)(2,1)}, u32[]{:S(2)}) copy-start(bf16[2,512,1536]{2,1,0:T(8,128)(2,1)} %get-tuple-element.8) | copy-start | bytes 9437188
  120.1 4.3 %copy-start = (bf16[64,1536]{1,0:T(8,128)(2,1)S(1)}, bf16[64,1536]{1,0:T(8,128)(2,1)}, u32[]{:S(2)}) copy-start(bf16[64,1536]{1,0:T(8,128)(2,1)} %get-tuple-element.12) | copy-start | bytes 589828
